TPU v7x, 512 devices: a whole 4x8x8 slice. The times are simulated.
512 devices in a mesh: ex: 8 (over z_lo, x), blk: 64 (over z_hi, y, core).
Axes of the slice: x: 4, y: 8, z: 8 (z_hi: 4, z_lo: 2; z = z_hi * 2 + z_lo), core: 2. Of those that a mesh axis runs over, the one named last changes fastest.
Arguments:
- activations: bfloat16 [1024, 28672], P('blk', 'ex'), may hold values from -6 to 6
- out_grads: bfloat16 [1024, 8192], P('ex', 'blk'), may hold values from -0.5 to 0.5
- basis_in: bfloat16 [28672, 28672], P('ex', 'blk'), may hold values from -0.03125 to 0.03125
- basis_out: bfloat16 [8192, 4096], P('blk', 'ex'), may hold values from -0.0625 to 0.0625
- example_ids: int32 [1024], replicated, may hold values from 0 to 8, as said below
Outputs:
- correction: float32 [4096, 28672], P('ex', 'blk')
Inputs may be any that keep to these rules, and one draw needn't show every extreme that they name: `example_ids`: example ids never fall along the tokens; every example 0 to 7 holds 1 to 192 tokens, and some example exactly 192; the id 8 marks padding tokens after the last example.
All inputs are finite; a program needn't handle non-finite values.
Results may differ from a plain program's by a relative error of at most 0.0029.
Values may be sent and summed in bfloat16 or wider, within the bound.
A program may use at most 64 MiB of HBM per device.

v0:
```python
import jax
import jax.numpy as jnp
from jax import lax
from jax.sharding import Mesh
from jax.sharding import PartitionSpec as P

LEN = 128
MOST = 192
BLK = ("blk_0", "blk_1", "blk_2")


def joined_along(parts, dim):
    parts = jnp.moveaxis(parts, 0, dim)
    dims = parts.shape
    return parts.reshape(*dims[:dim], dims[dim] * dims[dim + 1], *dims[dim + 2 :])


def copy_for_each(value, axis):
    devices = lax.axis_size(axis)
    return lax.all_to_all(
        jnp.broadcast_to(value[None], (devices, *value.shape)), axis, 0, 0, tiled=True
    )


def collect(value, axis, dim):
    return joined_along(copy_for_each(value, axis), dim)


def split_up(value, dim, devices):
    dims = value.shape
    parts = value.reshape(*dims[:dim], devices, dims[dim] // devices, *dims[dim + 1 :])
    return jnp.moveaxis(parts, dim, 0)


def summed_on_arrival(value, axis, dim):
    devices = lax.axis_size(axis)
    parts = lax.all_to_all(split_up(value, dim, devices), axis, 0, 0, tiled=True)
    return jnp.sum(parts, axis=0)


def filled_up(lines, devices):
    spare = -lines.shape[0] % devices
    if not spare:
        return lines
    return jnp.concatenate([lines, jnp.zeros((spare, *lines.shape[1:]), lines.dtype)])


def gather_axes(value, axes, dim):
    far, near = axes
    first = copy_for_each(value, far)
    parts = jnp.swapaxes(copy_for_each(first, near), 0, 1)
    return joined_along(parts.reshape(-1, *value.shape), dim)


def sum_by_axis(value, axes, dim):
    far, near = axes
    own = summed_on_arrival(split_up(value, dim, lax.axis_size(far)), near, dim + 1)
    return jnp.sum(lax.all_to_all(own, far, 0, 0, tiled=True), axis=0)


def nested_sum(value, axes):
    lines = value.reshape(-1, value.shape[-1])
    padded = filled_up(lines, lax.axis_size(axes[0]) * lax.axis_size(axes[1]))
    whole = gather_axes(sum_by_axis(padded, axes, 0), axes, 0)
    return lax.slice_in_dim(whole, 0, len(lines)).reshape(value.shape)


def local(activations, out_grads, basis_in, basis_out, example_ids):
    partial_in = jnp.dot(
        lax.all_gather(activations, BLK, axis=0, tiled=True),
        basis_in,
        preferred_element_type=jnp.float32,
    )
    grads_all = collect(out_grads, "ex", 0)
    share_in = summed_on_arrival(partial_in, "ex", 0).astype(jnp.bfloat16)
    proj_in = collect(share_in, "ex", 0)
    partial_out = jnp.dot(grads_all, basis_out, preferred_element_type=jnp.float32)
    proj_out = nested_sum(partial_out, (("blk_0", "blk_1"), "blk_2")).astype(jnp.bfloat16)
    token_count = example_ids.shape[0]
    example_count = token_count // LEN

    def add_example(example, running):
        offset = jnp.sum((example_ids < example).astype(jnp.int32))
        window_start = jnp.minimum(offset, token_count - MOST)
        window_ids = lax.dynamic_slice_in_dim(example_ids, window_start, MOST, 0)
        chosen = (window_ids == example).astype(proj_out.dtype)
        out_window = lax.dynamic_slice_in_dim(proj_out, window_start, MOST, 0) * chosen[:, None]
        in_window = lax.dynamic_slice_in_dim(proj_in, window_start, MOST, 0)
        example_grad = lax.dot_general(
            out_window, in_window, (((0,), (0,)), ((), ())), preferred_element_type=jnp.float32
        )
        return running + example_grad * example_grad

    initial = jnp.zeros((proj_out.shape[1], proj_in.shape[1]), jnp.float32)
    running = lax.fori_loop(0, example_count, add_example, initial)
    return running / example_count


def solution(mesh):
    finer = Mesh(mesh.devices.reshape(mesh.shape["ex"], 4, 8, 2), ("ex", "blk_0", "blk_1", "blk_2"))
    placed = (P(BLK, "ex"), P("ex", BLK), P("ex", BLK), P(BLK, "ex"), P())
    return jax.shard_map(
        local, mesh=finer, in_specs=placed, out_specs=P("ex", BLK), check_vma=False
    )
```

profile of v0, /device:TPU:1, one launch (start us, length us, event | category | flops | bytes accessed | tf_op | source)
XLA Modules:
  0.0 239.3 jit_solution(11566591690385458770)
XLA Ops:
  8.3 12.5 %all_to_all.35 = bf16[8,128,128]{2,1,0:T(8,128)(2,1)S(1)} all-to-all(bf16[8,128,128]{2,1,0:T(8,128)(2,1)S(1)} %broadcast_in_dim.13), channel_id=1, replica_groups=mesh['ex'=8,'blk_0'=4,'blk_1'=8,'blk_2'=2] {'ex'}, dimensions={0} | all-to-all | bytes 524288 | tf_op jit(solution)/shard_map/all_to_all | solution.py:20
  22.5 9.9 %all_to_all.36 = f32[2,32,16,512]{3,2,1,0:T(8,128)} all-to-all(f32[2,32,16,512]{3,2,1,0:T(8,128)S(1)} %copy.15), channel_id=1, replica_groups=mesh['ex'=8,'blk_0'=4,'blk_1'=8,'blk_2'=2] {'blk_2'}, dimensions={0} | all-to-all | bytes 4194304 | tf_op jit(solution)/shard_map/all_to_all | solution.py:37
  32.4 2.9 %reduce_sum.40 = f32[32,16,512]{2,1,0:T(8,128)} reduce(f32[2,32,16,512]{3,2,1,0:T(8,128)} %all_to_all.36, f32[]{:T(128)} %constant.34.clone.1), dimensions={0}, to_apply=%region_0.0 | reduce | flops 262144 | bytes 3145732 | tf_op jit(solution)/shard_map/reduce_sum | solution.py:38
  35.3 42.0 %all_to_all.37 = f32[32,16,512]{2,1,0:T(8,128)} all-to-all(f32[32,16,512]{2,1,0:T(8,128)} %reduce_sum.40), channel_id=1, replica_groups=mesh['ex'=8,'blk_0'=4,'blk_1'=8,'blk_2'=2] {'blk_0','blk_1'}, dimensions={0} | all-to-all | bytes 2097152 | tf_op jit(solution)/shard_map/all_to_all | solution.py:58
  79.4 9.3 %all-to-all-start.3 = ((bf16[32,16,512]{2,1,0:T(8,128)(2,1)}), bf16[32,16,512]{2,1,0:T(8,128)(2,1)}, u32[]{:S(2)}, u32[]{:S(2)}) async-start(bf16[32,16,512]{2,1,0:T(8,128)(2,1)} %broadcast_in_dim.14), calls=%async_computation.3 | async-start | bytes 1048576 | tf_op jit(solution)/shard_map/all_to_all | solution.py:20
  88.8 43.2 %all-gather.2.cloned.1.call-done = bf16[1024,3584]{1,0:T(8,128)(2,1)} async-done(((bf16[16,3584]{1,0:T(8,128)(2,1)}), bf16[1024,3584]{1,0:T(8,128)(2,1)}) %all-gather.2.cloned.1.call-update) | async-done | bytes 7340048 | tf_op jit(solution)/shard_map/all_gather | solution.py:70
  132.0 5.8 %convolution_bitcast_fusion.1 = f32[56,8,8,128]{3,2,1,0:T(8,128)S(1)} fusion(bf16[1024,3584]{1,0:T(8,128)(2,1)} %all-gather.2.cloned.1.call-done, bf16[3584,448]{0,1:T(8,128)(2,1)S(1)} %copy-done), kind=kOutput, calls=%fused_computation.12 | convolution fusion | flops 3288334336 | bytes 12386304 | tf_op jit(solution)/shard_map/dot_general | solution.py:69
  139.1 27.1 %all_to_all.38 = f32[8,128,448]{1,2,0:T(8,128)} all-to-all(f32[8,128,448]{1,2,0:T(8,128)} %bitcast.20), channel_id=1, replica_groups=mesh['ex'=8,'blk_0'=4,'blk_1'=8,'blk_2'=2] {'ex'}, dimensions={0} | all-to-all | bytes 3670016 | tf_op jit(solution)/shard_map/all_to_all | solution.py:37
  166.2 2.2 broadcast_in_dim.15
  168.3 6.6 %all-to-all-start.4 = ((bf16[2,32,16,512]{3,2,1,0:T(8,128)(2,1)}), bf16[2,32,16,512]{3,2,1,0:T(8,128)(2,1)}, u32[]{:S(2)}, u32[]{:S(2)}) async-start(bf16[2,32,16,512]{3,2,1,0:T(8,128)(2,1)} %broadcast_in_dim.15), calls=%async_computation.4 | async-start | bytes 2097152 | tf_op jit(solution)/shard_map/all_to_all | solution.py:20
  177.8 4.2 %all-to-all-start.6 = ((bf16[8,128,448]{1,2,0:T(8,128)(2,1)}), bf16[8,128,448]{1,2,0:T(8,128)(2,1)}, u32[]{:S(2)}, u32[]{:S(2)}) async-start(bf16[8,128,448]{1,2,0:T(8,128)(2,1)} %broadcast_in_dim.16), calls=%async_computation.6 | async-start | bytes 1835008 | tf_op jit(solution)/shard_map/all_to_all | solution.py:20
  182.1 2.3 copy.28
  184.4 11.3 %all-to-all-done.6 = bf16[8,128,448]{1,2,0:T(8,128)(2,1)} async-done(((bf16[8,128,448]{1,2,0:T(8,128)(2,1)}), bf16[8,128,448]{1,2,0:T(8,128)(2,1)}, u32[]{:S(2)}, u32[]{:S(2)}) %all-to-all-start.6) | async-done | bytes 917536 | tf_op jit(solution)/shard_map/all_to_all | solution.py:20
  195.7 2.3 copy.22
  197.9 32.3 %while.14 = (s32[]{:T(128)}, f32[512,448]{0,1:T(8,128)}, s32[1024]{0:T(1024)S(1)}, bf16[1024,512]{1,0:T(8,128)(2,1)}, bf16[1024,448]{1,0:T(8,128)(2,1)}, /*index=5*/s32[]{:T(128)}, s32[]{:T(128)}, s32[]{:T(128)}, s32[]{:T(128)}) while((s32[]{:T(128)}, f32[512,448]{0,1:T(8,128)}, s32[1024]{0:T(1024)S(1)}, ...), condition=%wide.region_5.0_spmd.clone, body=%wide.region_3.0_spmd.clone.sunk | while | flops 89165192 | bytes 2235564 | solution.py:95
  199.3 2.4 fusion.15
  203.0 2.7 %fusion.15 = f32[512,448]{0,1:T(8,128)} fusion(f32[512,448]{0,1:T(8,128)} %get-tuple-element.179, pred[]{:T(512)S(6)} %compare.3, bf16[1024,448]{1,0:T(8,128)(2,1)} %get-tuple-element.191, s32[]{:T(128)S(6)} %select_n.11, bf16[1024,512]{1,0:T(8,128)(2,1)} %get-tuple-element.190, bf16[192]{0:T(256)(128)(2,1)S(1)} %compare_convert_fusion.2), kind=kOutput, calls=%fused_computation.1.clone.1 | convolution fusion | flops 89161728 | bytes 2230144 | tf_op jit(solution)/shard_map/while/body/eval_jaxpr/dot_general | solution.py:89
  207.1 2.7 %fusion.15 = f32[512,448]{0,1:T(8,128)} fusion(f32[512,448]{0,1:T(8,128)} %get-tuple-element.179, pred[]{:T(512)S(6)} %compare.3, bf16[1024,448]{1,0:T(8,128)(2,1)} %get-tuple-element.191, s32[]{:T(128)S(6)} %select_n.11, bf16[1024,512]{1,0:T(8,128)(2,1)} %get-tuple-element.190, bf16[192]{0:T(256)(128)(2,1)S(1)} %compare_convert_fusion.2), kind=kOutput, calls=%fused_computation.1.clone.1 | convolution fusion | flops 89161728 | bytes 2230144 | tf_op jit(solution)/shard_map/while/body/eval_jaxpr/dot_general | solution.py:89
  211.2 2.7 %fusion.15 = f32[512,448]{0,1:T(8,128)} fusion(f32[512,448]{0,1:T(8,128)} %get-tuple-element.179, pred[]{:T(512)S(6)} %compare.3, bf16[1024,448]{1,0:T(8,128)(2,1)} %get-tuple-element.191, s32[]{:T(128)S(6)} %select_n.11, bf16[1024,512]{1,0:T(8,128)(2,1)} %get-tuple-element.190, bf16[192]{0:T(256)(128)(2,1)S(1)} %compare_convert_fusion.2), kind=kOutput, calls=%fused_computation.1.clone.1 | convolution fusion | flops 89161728 | bytes 2230144 | tf_op jit(solution)/shard_map/while/body/eval_jaxpr/dot_general | solution.py:89
  215.3 2.7 %fusion.15 = f32[512,448]{0,1:T(8,128)} fusion(f32[512,448]{0,1:T(8,128)} %get-tuple-element.179, pred[]{:T(512)S(6)} %compare.3, bf16[1024,448]{1,0:T(8,128)(2,1)} %get-tuple-element.191, s32[]{:T(128)S(6)} %select_n.11, bf16[1024,512]{1,0:T(8,128)(2,1)} %get-tuple-element.190, bf16[192]{0:T(256)(128)(2,1)S(1)} %compare_convert_fusion.2), kind=kOutput, calls=%fused_computation.1.clone.1 | convolution fusion | flops 89161728 | bytes 2230144 | tf_op jit(solution)/shard_map/while/body/eval_jaxpr/dot_general | solution.py:89
  219.3 2.7 %fusion.15 = f32[512,448]{0,1:T(8,128)} fusion(f32[512,448]{0,1:T(8,128)} %get-tuple-element.179, pred[]{:T(512)S(6)} %compare.3, bf16[1024,448]{1,0:T(8,128)(2,1)} %get-tuple-element.191, s32[]{:T(128)S(6)} %select_n.11, bf16[1024,512]{1,0:T(8,128)(2,1)} %get-tuple-element.190, bf16[192]{0:T(256)(128)(2,1)S(1)} %compare_convert_fusion.2), kind=kOutput, calls=%fused_computation.1.clone.1 | convolution fusion | flops 89161728 | bytes 2230144 | tf_op jit(solution)/shard_map/while/body/eval_jaxpr/dot_general | solution.py:89
  223.4 2.7 %fusion.15 = f32[512,448]{0,1:T(8,128)} fusion(f32[512,448]{0,1:T(8,128)} %get-tuple-element.179, pred[]{:T(512)S(6)} %compare.3, bf16[1024,448]{1,0:T(8,128)(2,1)} %get-tuple-element.191, s32[]{:T(128)S(6)} %select_n.11, bf16[1024,512]{1,0:T(8,128)(2,1)} %get-tuple-element.190, bf16[192]{0:T(256)(128)(2,1)S(1)} %compare_convert_fusion.2), kind=kOutput, calls=%fused_computation.1.clone.1 | convolution fusion | flops 89161728 | bytes 2230144 | tf_op jit(solution)/shard_map/while/body/eval_jaxpr/dot_general | solution.py:89
  227.5 2.7 %fusion.15 = f32[512,448]{0,1:T(8,128)} fusion(f32[512,448]{0,1:T(8,128)} %get-tuple-element.179, pred[]{:T(512)S(6)} %compare.3, bf16[1024,448]{1,0:T(8,128)(2,1)} %get-tuple-element.191, s32[]{:T(128)S(6)} %select_n.11, bf16[1024,512]{1,0:T(8,128)(2,1)} %get-tuple-element.190, bf16[192]{0:T(256)(128)(2,1)S(1)} %compare_convert_fusion.2), kind=kOutput, calls=%fused_computation.1.clone.1 | convolution fusion | flops 89161728 | bytes 2230144 | tf_op jit(solution)/shard_map/while/body/eval_jaxpr/dot_general | solution.py:89
  230.2 2.2 broadcast_multiply_fusion
  (33 shorter events, 15.7 us)
Async XLA Ops:
  6.5 125.4 %copy-start = (bf16[3584,448]{0,1:T(8,128)(2,1)S(1)}, bf16[3584,448]{0,1:T(8,128)(2,1)}, u32[]{:S(2)}) copy-start(bf16[3584,448]{0,1:T(8,128)(2,1)} %param.9) | copy-start | bytes 9633796
  6.5 125.4 %all-gather.2.cloned.1.call-start = ((), (), s32[]{:S(2)}) async-start(), calls=%async_computation.7 | async-start | bytes 7454720 | tf_op jit(solution)/shard_map/all_gather | solution.py:70
  79.4 59.6 %all-to-all-start.3 = ((bf16[32,16,512]{2,1,0:T(8,128)(2,1)}), bf16[32,16,512]{2,1,0:T(8,128)(2,1)}, u32[]{:S(2)}, u32[]{:S(2)}) async-start(bf16[32,16,512]{2,1,0:T(8,128)(2,1)} %broadcast_in_dim.14), calls=%async_computation.3 | async-start | bytes 1048576 | tf_op jit(solution)/shard_map/all_to_all | solution.py:20
  168.3 8.4 %all-to-all-start.4 = ((bf16[2,32,16,512]{3,2,1,0:T(8,128)(2,1)}), bf16[2,32,16,512]{3,2,1,0:T(8,128)(2,1)}, u32[]{:S(2)}, u32[]{:S(2)}) async-start(bf16[2,32,16,512]{3,2,1,0:T(8,128)(2,1)} %broadcast_in_dim.15), calls=%async_computation.4 | async-start | bytes 2097152 | tf_op jit(solution)/shard_map/all_to_all | solution.py:20
  176.5 21.4 %copy-start.1 = (s32[1024]{0:T(1024)S(1)}, s32[1024]{0:T(1024)}, u32[]{:S(2)}) copy-start(s32[1024]{0:T(1024)} %param.11) | copy-start | bytes 12292
  177.8 17.8 %all-to-all-start.6 = ((bf16[8,128,448]{1,2,0:T(8,128)(2,1)}), bf16[8,128,448]{1,2,0:T(8,128)(2,1)}, u32[]{:S(2)}, u32[]{:S(2)}) async-start(bf16[8,128,448]{1,2,0:T(8,128)(2,1)} %broadcast_in_dim.16), calls=%async_computation.6 | async-start | bytes 1835008 | tf_op jit(solution)/shard_map/all_to_all | solution.py:20
Sparse Core Ops, SparseCore 0:
  10.7 121.2 all-gather.1
where the time goes:
time: 240 us; the launch traced here: 239 us
  blocking collectives  91.6 us (38%)
  waiting for transfers between devices  55.5 us (23%)
  matrix products  28.5 us (12%)
  starting transfers between devices  20.1 us (8%)
  other arithmetic  13.9 us (6%)
  between operations  13.5 us (6%)
  local copies, waits for them, and re-layouts  11.3 us (5%)
  loops' own time  4.96 us (2%)
    all_gather x1, waiting for transfers between devices, local(): lax.all_gather(activations, BLK, axis=0, tiled=True)  43.2 us
    all_to_all x1, blocking collectives, sum_by_axis(): return jnp.sum(lax.all_to_all(own, far, 0, 0, tiled=True), axis=0)  42 us
    all_to_all x2, blocking collectives, summed_on_arrival(): lax.all_to_all(split_up(value, dim, devices), axis, 0, 0, tiled=True)  37 us
    dot_general x8, matrix products, add_example(): lax.dot_general(out_window, in_window, (((0,), (0,)), ((), ())), preferre...  21.4 us
    all_to_all x3, starting transfers between devices, copy_for_each(): lax.all_to_all(jnp.broadcast_to(value[None], (devices, *value.shape)), ax...  20.1 us
    all_to_all x1, blocking collectives, copy_for_each(): lax.all_to_all(jnp.broadcast_to(value[None], (devices, *value.shape)), ax...  12.5 us
    all_to_all x3, waiting for transfers between devices, copy_for_each(): lax.all_to_all(jnp.broadcast_to(value[None], (devices, *value.shape)), ax...  11.5 us
    dot_general x1, matrix products, local(): jnp.dot(lax.all_gather(activations, BLK, axis=0, tiled=True), basis_in, p...  5.76 us
  transfers between devices with their start and end apart: 4, of which 3 were waited for; matrix products, arithmetic and copies ran while one was open for 8% of the time, Pallas kernels for 0%

commit v1 on v0

v1 whole, which is shorter than its diff:
```python
import functools

import jax
import jax.numpy as jnp
from jax import lax
from jax.experimental import pallas as pl
from jax.experimental.pallas import tpu as pltpu
from jax.sharding import Mesh
from jax.sharding import PartitionSpec as P

AXES = ("zl", "x", "zh", "y", "c")
EX = ("zl", "x")
BLK = ("zh", "y", "c")
MESH = pl.DeviceIdType.MESH
MOST = 192
NX, NY, NZ, NE = 4, 8, 4, 8
ROWS = 16
BF = jnp.bfloat16
F32 = jnp.float32

Y_RATE = 46e3
Z_RATE = 23e3
X_RATE = 46e3
D_RATE = 600e3
LAG = 1.6


class Message:
    def __init__(self, link, nbytes, make, whole=None):
        self.link, self.nbytes, self.make, self.whole = link, nbytes, make, whole
        self.copies = None


class Task:
    def __init__(self, needs, sends, run=None, cost=0.05, after=(), rank=0):
        self.needs, self.sends, self.run = needs, sends, run
        self.cost, self.after, self.rank = cost, after, rank


def ordered(tasks, messages):
    rates = {"y+": Y_RATE, "y-": Y_RATE, "z+": Z_RATE, "z-": Z_RATE, "x": X_RATE, "d": D_RATE}
    free = dict.fromkeys(rates, 0.0)
    arrived, done, now, order = {}, {}, 0.0, []
    left = dict(tasks)
    while left:
        best = None
        for name, task in left.items():
            if any(m not in arrived for m in task.needs) or any(t not in done for t in task.after):
                continue
            ready = max([arrived[m] for m in task.needs] + [done[t] for t in task.after] + [0.0])
            key = (max(ready, now), task.rank, ready)
            if best is None or key < best[0]:
                best = (key, name)
        (start, _, _), name = best
        task = left.pop(name)
        now = start + task.cost
        done[name] = now
        for m in task.sends:
            message = messages[m]
            begin = max(now, free[message.link])
            free[message.link] = begin + message.nbytes / rates[message.link]
            arrived[m] = free[message.link] + LAG
        order.append(name)
    return order


def exchange(
    wide1,
    a_ref, g_ref, b_hbm, bo_ref, pi_ref, pall_ref,
    abuf, bbuf, gbuf, bobuf, pp, ring, zown, zbuf, part, mine, rsend, rbuf,
    ssem, rsem, bsem,
):
    zl, x, zh, y, c = (lax.axis_index(n) for n in AXES)
    e = zl * NX + x
    feats = a_ref.shape[1]
    outs = bo_ref.shape[1]
    width = b_hbm.shape[1]
    spans = ((0, wide1), (wide1, feats - wide1))

    def at_y(d):
        return (zl, x, zh, lax.rem(y + d + NY, NY), c)

    def at_z(d):
        return (zl, x, lax.rem(zh + d + NZ, NZ), y, c)

    def at_e(k, other=0):
        ek = lax.rem(e + k, NE)
        return (ek // NX, lax.rem(ek, NX), zh, y, lax.rem(c + other, 2))

    load_b = pltpu.make_async_copy(b_hbm, bbuf, bsem.at[0])
    load_b.start()

    partners = [at_y(1), at_y(-1), at_z(1), at_z(2), at_z(3)]
    partners += [at_e(k, o) for k in range(NE) for o in range(2) if (k, o) != (0, 0)]
    barrier = pltpu.get_barrier_semaphore()
    for device in partners:
        pl.semaphore_signal(barrier, inc=1, device_id=device, device_id_type=MESH)
    pl.semaphore_wait(barrier, len(partners))

    messages, tasks = {}, {}
    counts = [0, 0]

    def message(name, link, nbytes, parts, whole=None):
        arrival = counts[1]
        counts[1] += 1

        def make():
            copies = []
            for src, dst, device in parts():
                copies.append(
                    pltpu.make_async_remote_copy(
                        src_ref=src, dst_ref=dst,
                        send_sem=ssem.at[counts[0]], recv_sem=rsem.at[arrival],
                        device_id=device, device_id_type=MESH,
                    )
                )
                counts[0] += 1
            return copies

        messages[name] = Message(link, nbytes, make, None if whole is None else (whole, arrival))

    def a_slot(color, dy, dz, half=None, own=True):
        at, size = spans[color]
        if half is not None:
            size //= 2
            at += half * size
        cols = pl.ds(at, size)
        if own and (dy, dz) == (0, 0):
            return a_ref.at[:, cols], size
        return abuf.at[dy, 0, dz, :, cols], size

    def a_message(color, dy, dz, axis, sign, half=None):
        sy, sz = ((dy + sign) % NY, dz) if axis == "y" else (dy, (dz + sign) % NZ)
        size = a_slot(color, dy, dz, half)[1]
        device = at_y(sign) if axis == "y" else at_z(sign)
        name = ("a", color, dy, dz, half)
        message(
            name, axis + ("+" if sign > 0 else "-"), ROWS * size * 2,
            lambda: [(a_slot(color, sy, sz, half)[0], a_slot(color, dy, dz, half, False)[0], device)],
        )
        return name

    def along(color, axis, count, fixed):
        steps = {}
        for sign in (1, -1):
            chain = []
            for d in range(1, count // 2 + 1):
                place = (-sign * d) % count
                half = None if d < count // 2 else (0 if sign > 0 else 1)
                dy, dz = (place, fixed) if axis == "y" else (fixed, place)
                chain.append((a_message(color, dy, dz, axis, sign, half), (dy, dz)))
            steps[sign] = chain
        return steps

    first_sends = []
    filled = {(0, 0, 0): [], (1, 0, 0): []}
    starts = {}

    def ring_tasks(color, axis, fixed, from_task, rank):
        steps = along(color, axis, NY if axis == "y" else NZ, fixed)
        for sign in (1, -1):
            chain = steps[sign]
            for (name, place), (following, _) in zip(chain, chain[1:]):
                tasks[("fwd", name)] = Task([name], [following], rank=rank)
            for name, place in chain:
                filled.setdefault((color, *place), []).append(name)
        return [steps[1][0][0], steps[-1][0][0]]

    if True:
        own_sends = []
        own_sends += ring_tasks(0, "z", 0, None, 0)
        for dz in (0, 1, 3, 2):
            sends = ring_tasks(0, "y", dz, None, 1)
            if dz == 0:
                own_sends += sends
            else:
                starts[(0, 0, dz)] = sends
        sends = ring_tasks(1, "y", 0, None, 0)
        own_sends += sends
        for dy in (0, 1, 7, 2, 6, 3, 5, 4):
            sends = ring_tasks(1, "z", dy, None, 1)
            if dy == 0:
                own_sends += sends
            else:
                starts[(1, dy, 0)] = sends
        for place, sends in starts.items():
            tasks[("go", place)] = Task(filled[place], sends, rank=1)

    for dy in range(NY):
        for color in range(2):
            cols = pl.ds(*spans[color])
            piece = lambda slot, dy=dy, cols=cols: abuf.at[dy, slot, :, :, cols]
            message(
                ("d", color, dy), "d", NZ * ROWS * spans[color][1] * 2,
                lambda piece=piece: [(piece(0), piece(1), at_e(0, 1))],
            )
            needs = sum((filled[(color, dy, dz)] for dz in range(NZ)), [])
            tasks[("share", color, dy)] = Task(needs, [("d", color, dy)], after=["start"], rank=2)

    gr = g_ref.shape[0] // 2
    gk = g_ref.shape[1]

    def g_parts():
        for k in range(NE):
            for o in range(2):
                if (k, o) != (0, 0):
                    rows = pl.multiple_of(lax.rem(c + o, 2) * gr, gr)
                    yield (
                        g_ref.at[pl.ds(rows, gr), :],
                        gbuf.at[pl.ds(pl.multiple_of(e * gr, gr), gr), pl.ds(o * gk, gk)],
                        at_e(k, o),
                    )

    message("g", "x", 15 * gr * gk, lambda: list(g_parts()), gbuf.at[pl.ds(0, 15 * gr // 2), :])
    message("bo", "d", gk * outs * 2, lambda: [(bo_ref, bobuf.at[pl.ds(gk, gk), :], at_e(0, 1))])

    half_outs = outs // 2
    for sign in (1, -1):
        for s in range(NY // 2):
            slot = ring.at[0 if sign > 0 else 1, s]
            if s == 0:
                cols = pl.ds(0 if sign > 0 else half_outs, half_outs)
                src = pp.at[lax.rem(y + NY // 2, NY), :, cols]
                parts = lambda src=src, dst=slot.at[:, cols], sign=sign: [(src, dst, at_y(sign))]
            else:
                src = ring.at[0 if sign > 0 else 1, s - 1]
                parts = lambda src=src, dst=slot, sign=sign: [(src, dst, at_y(sign))]
            message(("p", sign, s), "y+" if sign > 0 else "y-", gr * outs * (2 if s == 0 else 4), parts)

    def project_out():
        total = jnp.dot(gbuf[...], bobuf[...], preferred_element_type=F32)
        pp[...] = total.reshape(pp.shape)

    tasks["p0"] = Task(["g", "bo"], [("p", 1, 0), ("p", -1, 0)], project_out, 0.8, ["start"])
    for sign in (1, -1):
        for s in range(1, NY // 2):

            def add(sign=sign, s=s):
                index = 0 if sign > 0 else 1
                own = pp.at[lax.rem(y + sign * (NY // 2 - s) + NY, NY)]
                if s == 1:
                    near = pl.ds(0 if sign > 0 else half_outs, half_outs)
                    far = pl.ds(half_outs if sign > 0 else 0, half_outs)
                    ring[index, s - 1, :, near] = ring[index, s - 1, :, near] + own[:, near]
                    ring[index, s - 1, :, far] = own[:, far]
                else:
                    ring[index, s - 1] = ring[index, s - 1] + own[...]

            tasks[("padd", sign, s)] = Task([("p", sign, s - 1)], [("p", sign, s)], add, 0.15, ["p0"])

    def sum_y():
        zown[...] = (pp[y] + ring[0, NY // 2 - 1] + ring[1, NY // 2 - 1]).reshape(zown.shape)

    message(
        "pz", "z+", 4 * ROWS * outs * 4,
        lambda: [(zown.at[lax.rem(zh + k, NZ)], zbuf.at[k - 1], at_z(k)) for k in range(1, NZ)],
        zbuf,
    )
    tasks["psum"] = Task([("p", 1, NY // 2 - 1), ("p", -1, NY // 2 - 1)], ["pz"], sum_y, 0.2, ["p0"])

    def finish_p():
        total = zown[zh] + zbuf[0] + zbuf[1] + zbuf[2]
        pall_ref[y, c, zh] = total.astype(BF)

    message(
        "pgz", "z+", 4 * ROWS * outs * 2,
        lambda: [(pall_ref.at[y, c, zh], pall_ref.at[y, c, zh], at_z(k)) for k in range(1, NZ)],
        pall_ref.at[0, 0, pl.ds(0, NZ - 1)],
    )
    tasks["pfin"] = Task(["pz"], ["pgz"], finish_p, 0.1, ["psum"])
    for sign in (1, -1):
        for s in range(NY // 2):
            rows = pl.ds(0, NZ) if s < NY // 2 - 1 else pl.ds(0 if sign > 0 else NZ // 2, NZ // 2)
            place = pall_ref.at[lax.rem(y - sign * s + NY, NY), c, rows]
            message(
                ("pg", sign, s), "y+" if sign > 0 else "y-", gr * outs * 2 // (1 if s < NY // 2 - 1 else 2),
                lambda place=place, sign=sign: [(place, place, at_y(sign))],
            )
    for off in range(NY):
        place = pall_ref.at[lax.rem(y + off, NY), c]
        message(("pd", off), "d", gr * outs * 2, lambda place=place: [(place, place, at_e(0, 1))])
    tasks[("pgo", 0)] = Task(["pgz"], [("pg", 1, 0), ("pg", -1, 0), ("pd", 0)], after=["pfin"])
    for s in range(1, NY // 2):
        for sign in (1, -1):
            tasks[("pgo", s, sign)] = Task(
                [("pg", sign, s - 1)], [("pg", sign, s), ("pd", (-sign * s) % NY)], after=["pfin"]
            )
    far = NY // 2
    tasks[("pgo", far)] = Task([("pg", 1, far - 1), ("pg", -1, far - 1)], [("pd", far)], after=["pfin"])

    def own_place(dy):
        core = lax.rem(c + e // NZ, 2)
        return lax.rem(zh + lax.rem(e, NZ), NZ) * (NY * 2) + lax.rem(y + dy, NY) * 2 + core

    tile = 512
    for dy in range(NY):

        def project_in(dy=dy):
            part[...] = jnp.zeros_like(part)

            @pl.loop(0, feats // tile)
            def _(t):
                cols = pl.ds(pl.multiple_of(t * tile, tile), tile)
                rows = abuf[dy, :, :, :, cols].reshape(2 * NZ * ROWS, tile)
                part[...] += jnp.dot(rows, bbuf[cols, :], preferred_element_type=F32)

            mine[dy] = part[pl.ds(pl.multiple_of(e * ROWS, ROWS), ROWS), :]
            rsend[dy] = part[...].reshape(NE, ROWS, width).astype(BF)

        def sum_in(dy=dy):
            total = mine[dy]
            for k in range(NE - 1):
                total = total + rbuf[dy, k].astype(F32)
            pi_ref[own_place(dy)] = total.astype(BF)

        message(
            ("rs", dy), "x", 8 * ROWS * width,
            lambda dy=dy: [
                (rsend.at[dy, lax.rem(e + k, NE)], rbuf.at[dy, k - 1], at_e(k)) for k in range(1, NE)
            ],
            rbuf.at[dy],
        )
        message(
            ("ag", dy), "x", 8 * ROWS * width,
            lambda dy=dy: [
                (pi_ref.at[own_place(dy)], pi_ref.at[own_place(dy)], at_e(k)) for k in range(1, NE)
            ],
            pi_ref.at[pl.ds(0, NE - 1)],
        )
        shared = [("share", color, dy) for color in range(2)]
        tasks[("mm", dy)] = Task(
            [("d", 0, dy), ("d", 1, dy)], [("rs", dy)], project_in, 1.0, ["start", *shared], rank=3
        )
        tasks[("sum", dy)] = Task([("rs", dy)], [("ag", dy)], sum_in, 0.2, [("mm", dy)], rank=2)

    def begin():
        abuf[0, 0, 0] = a_ref[...]
        gbuf[pl.ds(pl.multiple_of(e * gr, gr), gr), pl.ds(0, gk)] = g_ref[pl.ds(pl.multiple_of(c * gr, gr), gr), :]
        bobuf[pl.ds(0, gk), :] = bo_ref[...]

    tasks["start"] = Task([], ["g", "bo", *own_sends], begin, 0.3)
    for name, task in tasks.items():
        if name != "start" and not task.needs and not task.after:
            task.after = ["start"]

    waited = set()
    started = []

    def wait_for(name):
        if name in waited:
            return
        waited.add(name)
        item = messages[name]
        if item.whole is None:
            item.copies[0].wait_recv()
        else:
            ref, index = item.whole
            pltpu.make_async_copy(ref, ref, rsem.at[index]).wait()

    loaded = False
    for name in ordered(tasks, messages):
        task = tasks[name]
        for m in task.needs:
            wait_for(m)
        if name == "start":
            for m in task.sends:
                item = messages[m]
                item.copies = item.make()
                for copy in item.copies:
                    copy.start()
                started.append(item)
            task.run()
            continue
        if name[0] == "mm" and not loaded:
            load_b.wait()
            loaded = True
        if task.run is not None:
            task.run()
        for m in task.sends:
            item = messages[m]
            item.copies = item.make()
            for copy in item.copies:
                copy.start()
            started.append(item)
    for name in messages:
        wait_for(name)
    for item in started:
        for copy in item.copies:
            copy.wait_send()


def combine(ids_ref, pout_ref, pin_ref, out_ref):
    tokens = pin_ref.shape[0]
    examples = NE
    window = MOST + ROWS
    ids = ids_ref[...]
    bounds = [jnp.sum((ids < n).astype(jnp.int32)) for n in range(examples + 1)]
    for n in range(examples):
        begin, end = bounds[n], bounds[n + 1]
        start = jnp.minimum((begin // ROWS) * ROWS, tokens - window)
        start = pl.multiple_of(start, ROWS)
        place = start + lax.broadcasted_iota(jnp.int32, (window, 1), 0)
        keep = (place >= begin) & (place < end)
        left = jnp.where(keep, pout_ref[pl.ds(start, window), :], 0)
        grad = lax.dot_general(
            left, pin_ref[pl.ds(start, window), :], (((0,), (0,)), ((), ())), preferred_element_type=F32
        )
        if n == 0:
            out_ref[...] = grad * grad
        elif n < examples - 1:
            out_ref[...] += grad * grad
        else:
            out_ref[...] = (out_ref[...] + grad * grad) * (1.0 / examples)


def local(activations, out_grads, basis_in, basis_out, example_ids):
    feats, width = basis_in.shape
    outs = basis_out.shape[1]
    tokens = example_ids.shape[0]
    gk = out_grads.shape[1]
    gr = out_grads.shape[0] // 2
    vmem = pl.BlockSpec(memory_space=pltpu.VMEM)
    wide1 = (feats * 22 // 28) // 256 * 256
    proj_in, proj_out = pl.pallas_call(
        functools.partial(exchange, wide1),
        out_shape=(
            jax.ShapeDtypeStruct((tokens // ROWS, ROWS, width), BF),
            jax.ShapeDtypeStruct((NY, 2, NZ, ROWS, outs), BF),
        ),
        in_specs=[vmem, vmem, pl.BlockSpec(memory_space=pl.ANY), vmem],
        out_specs=(vmem, vmem),
        scratch_shapes=[
            pltpu.VMEM((NY, 2, NZ, ROWS, feats), BF),
            pltpu.VMEM((feats, width), BF),
            pltpu.VMEM((NE * gr, 2 * gk), BF),
            pltpu.VMEM((2 * gk, outs), BF),
            pltpu.VMEM((NY, gr, outs), F32),
            pltpu.VMEM((2, NY // 2, gr, outs), F32),
            pltpu.VMEM((NZ, ROWS, outs), F32),
            pltpu.VMEM((NZ - 1, ROWS, outs), F32),
            pltpu.VMEM((2 * NZ * ROWS, width), F32),
            pltpu.VMEM((NY, ROWS, width), F32),
            pltpu.VMEM((NY, NE, ROWS, width), BF),
            pltpu.VMEM((NY, NE - 1, ROWS, width), BF),
            pltpu.SemaphoreType.DMA((256,)),
            pltpu.SemaphoreType.DMA((160,)),
            pltpu.SemaphoreType.DMA((1,)),
        ],
        compiler_params=pltpu.CompilerParams(
            collective_id=0, has_side_effects=True, vmem_limit_bytes=48 << 20
        ),
        name="exchange",
    )(activations, out_grads, basis_in, basis_out)
    return pl.pallas_call(
        combine,
        out_shape=jax.ShapeDtypeStruct((outs, width), F32),
        in_specs=[vmem] * 3,
        out_specs=vmem,
        compiler_params=pltpu.CompilerParams(vmem_limit_bytes=48 << 20),
        name="combine",
    )(example_ids.reshape(-1, 128), proj_out.reshape(tokens, outs), proj_in.reshape(tokens, width))


def solution(mesh):
    finer = Mesh(mesh.devices.reshape(2, NX, NZ, NY, 2), AXES)
    placed = (P(BLK, EX), P(EX, BLK), P(EX, BLK), P(BLK, EX), P())
    return jax.shard_map(local, mesh=finer, in_specs=placed, out_specs=P(EX, BLK), check_vma=False)
```

time: 240 us -> 109 us (0.45)
  Pallas kernels: 0 us -> 100 us
  blocking collectives: 91.6 us -> 0 us
  waiting for transfers between devices: 55.5 us -> 0 us
  matrix products: 28.5 us -> 0 us
  starting transfers between devices: 20.1 us -> 0 us
  other arithmetic: 13.9 us -> 0 us
  between operations: 13.5 us -> 0.04 us
  loops' own time: 4.96 us -> 0 us
    pallas_call x0 -> x2, Pallas kernels: none -> 100 us  [the longest x1 98.3 us: local(): pl.pallas_call(functools.partial(exchange, wide1), out_shape=(jax.ShapeDt...]
    all_to_all x4 -> x0, blocking collectives: 91.6 us -> none  [the longest x1 42 us: sum_by_axis(): return jnp.sum(lax.all_to_all(own, far, 0, 0, tiled=True), axis=0)]
    all_gather x1 -> x0, waiting for transfers between devices: 43.2 us -> none  [local(): lax.all_gather(activations, BLK, axis=0, tiled=True)]
    dot_general x10 -> x0, matrix products: 28.5 us -> none  [the longest x8 21.4 us: add_example(): lax.dot_general(out_window, in_window, (((0,), (0,)), ((), ())), preferre...]
    all_to_all x3 -> x0, starting transfers between devices: 20.1 us -> none  [copy_for_each(): lax.all_to_all(jnp.broadcast_to(value[None], (devices, *value.shape)), ax...]
    all_to_all x3 -> x0, waiting for transfers between devices: 11.5 us -> none  [copy_for_each(): lax.all_to_all(jnp.broadcast_to(value[None], (devices, *value.shape)), ax...]
    reduce_sum x11 -> x0, other arithmetic: 11 us -> none  [the longest x8 5.29 us: add_example(): offset = jnp.sum((example_ids < example).astype(jnp.int32))]
    unnamed x5 -> x11, local copies, waits for them, and re-layouts: 2.27 us -> 7.8 us
  transfers between devices with their start and end apart: 4 -> 0, of which waited for: 3 -> 0; matrix products, arithmetic and copies ran while one was open for 8% -> 0% of each run, Pallas kernels for 0% -> 0%
where the time goes in v1:
time: 109 us
  Pallas kernels  100 us (92%)
  local copies, waits for them, and re-layouts  9.04 us (8%)
    pallas_call x1, Pallas kernels, local(): pl.pallas_call(functools.partial(exchange, wide1), out_shape=(jax.ShapeDt...  98.3 us
    unnamed x11, local copies, waits for them, and re-layouts  7.8 us

profile of v1, /device:TPU:1, one launch (start us, length us, event | category | flops | bytes accessed | tf_op | source)
XLA Modules:
  0.0 109.2 jit_solution(16948493058439055887)
XLA Ops:
  0.0 0.0 copy-start.1
  0.0 0.0 copy-start.3
  0.0 0.0 copy-start.2
  0.0 5.8 %copy.6.b_hbm = bf16[3584,448]{1,0:T(8,128)(2,1)} copy(bf16[3584,448]{0,1:T(8,128)(2,1)} %param.7) | data formatting | bytes 6422528 | tf_op args[2]
  5.8 0.0 copy-done.1
  5.8 0.0 copy-done.3
  5.8 0.0 copy-done.2
  5.8 0.0 copy-start
  5.8 2.0 %copy-done = bf16[3584,448]{1,0:T(8,128)(2,1)S(1)} copy-done((bf16[3584,448]{1,0:T(8,128)(2,1)S(1)}, bf16[3584,448]{1,0:T(8,128)(2,1)}, u32[]{:S(2)}) %copy-start) | copy-done | bytes 3211288
  7.8 0.0 copy-start.4
  7.8 98.3 %exchange.1 = (bf16[64,16,448]{2,1,0:T(8,128)(2,1)S(1)}, bf16[8,2,4,16,512]{4,3,2,1,0:T(8,128)(2,1)S(1)}) custom-call(bf16[16,3584]{1,0:T(8,128)(2,1)S(1)} %copy-done.2, bf16[128,128]{1,0:T(8,128)(2,1)S(1)} %copy-done.3, bf16[3584,448]{1,0:T(8,128)(2,1)S(1)} %copy-done, bf16[128,512]{1,0:T(8,128)(2,1)S(1)} %copy-done.1), custom_call_target="tpu_custom_call" | custom-call | tf_op jit(solution)/shard_map/exchange/pallas_call | solution.py:424
  106.2 0.0 copy-done.4
  106.2 1.8 %combine.1 = f32[512,448]{1,0:T(8,128)S(1)} custom-call(s32[8,128]{1,0:T(8,128)S(1)} %bitcast.5, bf16[1024,512]{1,0:T(8,128)(2,1)S(1)} %bitcast.4, bf16[1024,448]{1,0:T(8,128)(2,1)S(1)} %bitcast.3), custom_call_target="tpu_custom_call" | custom-call | tf_op jit(solution)/shard_map/combine/pallas_call | solution.py:454
  107.9 1.2 %copy.7 = f32[512,448]{0,1:T(8,128)} copy(f32[512,448]{1,0:T(8,128)S(1)} %combine.1) | data formatting | bytes 1835008 | tf_op jit(solution)/shard_map/combine/pallas_call | solution.py:454
Async XLA Ops:
  0.0 5.8 %copy-start.1 = (bf16[128,512]{1,0:T(8,128)(2,1)S(1)}, bf16[128,512]{1,0:T(8,128)(2,1)}, u32[]{:S(2)}) copy-start(bf16[128,512]{1,0:T(8,128)(2,1)} %bo_ref.1) | copy-start | bytes 393220
  0.0 5.8 %copy-start.3 = (bf16[128,128]{1,0:T(8,128)(2,1)S(1)}, bf16[128,128]{1,0:T(8,128)(2,1)}, u32[]{:S(2)}) copy-start(bf16[128,128]{1,0:T(8,128)(2,1)} %g_ref.1) | copy-start | bytes 98308
  0.0 5.8 %copy-start.2 = (bf16[16,3584]{1,0:T(8,128)(2,1)S(1)}, bf16[16,3584]{1,0:T(8,128)(2,1)}, u32[]{:S(2)}) copy-start(bf16[16,3584]{1,0:T(8,128)(2,1)} %a_ref.1) | copy-start | bytes 344068
  5.8 2.0 %copy-start = (bf16[3584,448]{1,0:T(8,128)(2,1)S(1)}, bf16[3584,448]{1,0:T(8,128)(2,1)}, u32[]{:S(2)}) copy-start(bf16[3584,448]{1,0:T(8,128)(2,1)} %copy.6.b_hbm) | copy-start | bytes 9633796
  7.8 98.3 %copy-start.4 = (s32[1024]{0:T(1024)S(1)}, s32[1024]{0:T(1024)}, u32[]{:S(2)}) copy-start(s32[1024]{0:T(1024)} %param.9) | copy-start | bytes 12292

commit v2 on v1

v2 whole, which is shorter than its diff:
```python
import functools

import jax
import jax.numpy as jnp
from jax import lax
from jax.experimental import pallas as pl
from jax.experimental.pallas import tpu as pltpu
from jax.sharding import Mesh
from jax.sharding import PartitionSpec as P

AXES = ("zl", "x", "zh", "y", "c")
EX = ("zl", "x")
BLK = ("zh", "y", "c")
MESH = pl.DeviceIdType.MESH
MOST = 192
NX, NY, NZ, NE = 4, 8, 4, 8
ROWS = 16
BF = jnp.bfloat16
F32 = jnp.float32

RATE = {"y+": 40e3, "y-": 40e3, "z+": 16e3, "z-": 16e3, "x": 46e3, "d": 600e3}
LAG = {"y+": 3.0, "y-": 3.0, "z+": 4.0, "z-": 4.0, "x": 5.0, "d": 2.0}
BACKLOG = 1.0


class Message:
    def __init__(self, link, nbytes, make, whole, rank):
        self.link, self.nbytes, self.make, self.whole, self.rank = link, nbytes, make, whole, rank
        self.copies = None


class Task:
    def __init__(self, needs, sends, run=None, cost=0.05, after=(), rank=0):
        self.needs, self.sends, self.run = needs, sends, run
        self.cost, self.after, self.rank = cost, after, rank


def ordered(tasks, messages):
    free = dict.fromkeys(RATE, 0.0)
    arrived, done, now, order = {}, {}, 0.0, []
    left, pending = dict(tasks), []
    while left or pending:
        moments = []
        for number, (rank, m) in enumerate(pending):
            when = free[messages[m].link] - BACKLOG
            moments.append((max(when, now), 0, rank, number, m))
        for number, (name, task) in enumerate(left.items()):
            if any(m not in arrived for m in task.needs) or any(t not in done for t in task.after):
                continue
            ready = max([arrived[m] for m in task.needs] + [done[t] for t in task.after] + [0.0])
            moments.append((max(ready, now), 1, (task.rank, ready), number, name))
        now, is_task, key, _, name = min(moments, key=lambda moment: moment[:4])
        if is_task:
            task = left.pop(name)
            now += task.cost
            done[name] = now
            pending += [(messages[m].rank, m) for m in task.sends]
        else:
            pending.remove((key, name))
            message = messages[name]
            free[message.link] = max(now, free[message.link]) + message.nbytes / RATE[message.link]
            arrived[name] = free[message.link] + LAG[message.link]
            now += 0.03
        order.append((is_task, name))
    return order


def exchange(
    wide1,
    a_ref, g_ref, b_hbm, bo_ref, ids_ref, out_ref,
    pi_ref, pall_ref, abuf, bbuf, gbuf, bobuf, pp, ring, zown, zbuf, part, mine, rsend, rbuf,
    ssem, rsem, bsem,
):
    zl, x, zh, y, c = (lax.axis_index(n) for n in AXES)
    e = zl * NX + x
    feats = a_ref.shape[1]
    outs = bo_ref.shape[1]
    width = b_hbm.shape[0]
    spans = ((0, wide1), (wide1, feats - wide1))

    def at_y(d):
        return (zl, x, zh, lax.rem(y + d + NY, NY), c)

    def at_z(d):
        return (zl, x, lax.rem(zh + d + NZ, NZ), y, c)

    def at_e(k, other=0):
        ek = lax.rem(e + k, NE)
        return (ek // NX, lax.rem(ek, NX), zh, y, lax.rem(c + other, 2))

    load_b = pltpu.make_async_copy(b_hbm, bbuf, bsem.at[0])
    load_b.start()

    partners = [at_y(1), at_y(-1), at_z(1), at_z(2), at_z(3)]
    partners += [at_e(k, o) for k in range(NE) for o in range(2) if (k, o) != (0, 0)]
    barrier = pltpu.get_barrier_semaphore()
    for device in partners:
        pl.semaphore_signal(barrier, inc=1, device_id=device, device_id_type=MESH)
    pl.semaphore_wait(barrier, len(partners))

    messages, tasks = {}, {}
    counts = [0, 0]

    def message(name, link, nbytes, parts, whole=None, rank=1):
        arrival = counts[1]
        counts[1] += 1

        def make():
            copies = []
            for src, dst, device in parts():
                copies.append(
                    pltpu.make_async_remote_copy(
                        src_ref=src, dst_ref=dst,
                        send_sem=ssem.at[counts[0]], recv_sem=rsem.at[arrival],
                        device_id=device, device_id_type=MESH,
                    )
                )
                counts[0] += 1
            return copies

        rank = 0 if name[0] in "pg" else rank
        messages[name] = Message(link, nbytes, make, None if whole is None else (whole, arrival), rank)

    def a_slot(color, dy, dz, half=None, own=True):
        at, size = spans[color]
        if half is not None:
            size //= 2
            at += half * size
        cols = pl.ds(at, size)
        if own and (dy, dz) == (0, 0):
            return a_ref.at[:, cols], size
        return abuf.at[dy, 0, dz, :, cols], size

    def a_message(color, dy, dz, axis, sign, half=None):
        sy, sz = ((dy + sign) % NY, dz) if axis == "y" else (dy, (dz + sign) % NZ)
        size = a_slot(color, dy, dz, half)[1]
        device = at_y(sign) if axis == "y" else at_z(sign)
        name = ("a", color, dy, dz, half)
        message(
            name, axis + ("+" if sign > 0 else "-"), ROWS * size * 2,
            lambda: [(a_slot(color, sy, sz, half)[0], a_slot(color, dy, dz, half, False)[0], device)],
        )
        return name

    def along(color, axis, count, fixed):
        steps = {}
        for sign in (1, -1):
            chain = []
            for d in range(1, count // 2 + 1):
                place = (-sign * d) % count
                half = None if d < count // 2 else (0 if sign > 0 else 1)
                dy, dz = (place, fixed) if axis == "y" else (fixed, place)
                chain.append((a_message(color, dy, dz, axis, sign, half), (dy, dz)))
            steps[sign] = chain
        return steps

    first_sends = []
    filled = {(0, 0, 0): [], (1, 0, 0): []}
    starts = {}

    def ring_tasks(color, axis, fixed, from_task, rank):
        steps = along(color, axis, NY if axis == "y" else NZ, fixed)
        for sign in (1, -1):
            chain = steps[sign]
            for (name, place), (following, _) in zip(chain, chain[1:]):
                tasks[("fwd", name)] = Task([name], [following], rank=rank)
            for name, place in chain:
                filled.setdefault((color, *place), []).append(name)
        return [steps[1][0][0], steps[-1][0][0]]

    if True:
        own_sends = []
        own_sends += ring_tasks(0, "z", 0, None, 0)
        for dz in (0, 1, 3, 2):
            sends = ring_tasks(0, "y", dz, None, 1)
            if dz == 0:
                own_sends += sends
            else:
                starts[(0, 0, dz)] = sends
        sends = ring_tasks(1, "y", 0, None, 0)
        own_sends += sends
        for dy in (0, 1, 7, 2, 6, 3, 5, 4):
            sends = ring_tasks(1, "z", dy, None, 1)
            if dy == 0:
                own_sends += sends
            else:
                starts[(1, dy, 0)] = sends
        for place, sends in starts.items():
            tasks[("go", place)] = Task(filled[place], sends, rank=1)

    for dy in range(NY):
        for color in range(2):
            cols = pl.ds(*spans[color])
            piece = lambda slot, dy=dy, cols=cols: abuf.at[dy, slot, :, :, cols]
            message(
                ("d", color, dy), "d", NZ * ROWS * spans[color][1] * 2,
                lambda piece=piece: [(piece(0), piece(1), at_e(0, 1))],
            )
            needs = sum((filled[(color, dy, dz)] for dz in range(NZ)), [])
            tasks[("share", color, dy)] = Task(needs, [("d", color, dy)], after=["place"], rank=2)

    gr = g_ref.shape[0] // 2
    gk = g_ref.shape[1]

    def g_parts():
        for k in range(NE):
            for o in range(2):
                if (k, o) != (0, 0):
                    rows = pl.multiple_of(lax.rem(c + o, 2) * gr, gr)
                    yield (
                        g_ref.at[pl.ds(rows, gr), :],
                        gbuf.at[pl.ds(pl.multiple_of(e * gr, gr), gr), pl.ds(o * gk, gk)],
                        at_e(k, o),
                    )

    message("g", "x", 15 * gr * gk, lambda: list(g_parts()), gbuf.at[pl.ds(0, 15 * gr // 2), :])
    message("bo", "d", gk * outs * 2, lambda: [(bo_ref, bobuf.at[pl.ds(gk, gk), :], at_e(0, 1))])

    half_outs = outs // 2
    lanes = outs // 2
    p_starts = []
    for sign in (1, -1):
        side = 0 if sign > 0 else 1
        for lane in range(2):
            cols = pl.ds(lane * lanes, lanes)
            first = 0 if lane == side else 1
            for s in range(first, NY // 2):
                if s == first:
                    src = pp.at[lax.rem(y + sign * (NY // 2 - s) + NY, NY), :, cols]
                    p_starts.append(("p", sign, lane, s))
                else:
                    src = ring.at[side, s - 1, :, cols]
                message(
                    ("p", sign, lane, s), "y+" if sign > 0 else "y-", gr * lanes * 4,
                    lambda src=src, dst=ring.at[side, s, :, cols], sign=sign: [(src, dst, at_y(sign))],
                )

    def project_out():
        total = jnp.dot(gbuf[...], bobuf[...], preferred_element_type=F32)
        pp[...] = total.reshape(pp.shape)

    tasks["p0"] = Task(["g", "bo"], p_starts, project_out, 0.8, ["place"])
    for sign in (1, -1):
        side = 0 if sign > 0 else 1
        for lane in range(2):
            for s in range(1 if lane == side else 2, NY // 2):

                def add(sign=sign, side=side, cols=pl.ds(lane * lanes, lanes), s=s):
                    own = pp.at[lax.rem(y + sign * (NY // 2 - s) + NY, NY), :, cols]
                    ring[side, s - 1, :, cols] = ring[side, s - 1, :, cols] + own[...]

                tasks[("padd", sign, lane, s)] = Task(
                    [("p", sign, lane, s - 1)], [("p", sign, lane, s)], add, 0.1, ["p0"]
                )

    def sum_y():
        zown[...] = (pp[y] + ring[0, NY // 2 - 1] + ring[1, NY // 2 - 1]).reshape(zown.shape)

    message(
        "pz", "z+", 2 * ROWS * outs * 4,
        lambda: [(zown.at[lax.rem(zh + k, NZ)], zbuf.at[k - 1], at_z(k)) for k in range(1, NZ)],
        zbuf,
    )
    last = [("p", sign, lane, NY // 2 - 1) for sign in (1, -1) for lane in range(2)]
    tasks["psum"] = Task(last, ["pz"], sum_y, 0.2, ["p0"])

    def p_place(at):
        return at * (2 * NZ) + c * NZ

    def finish_p():
        total = zown[zh] + zbuf[0] + zbuf[1] + zbuf[2]
        pall_ref[p_place(y) + zh] = total.astype(BF)

    message(
        "pgz", "z+", 2 * ROWS * outs * 2,
        lambda: [(pall_ref.at[p_place(y) + zh], pall_ref.at[p_place(y) + zh], at_z(k)) for k in range(1, NZ)],
        pall_ref.at[pl.ds(0, NZ - 1)],
    )
    tasks["pfin"] = Task(["pz"], ["pgz"], finish_p, 0.1, ["psum"])
    piece = NZ // 2
    p_filled = {off: [] for off in range(NY)}
    p_goes = []
    for sign in (1, -1):
        side = 0 if sign > 0 else 1
        for lane in range(2):
            hops = NY // 2 if lane == side else NY // 2 - 1
            for s in range(hops):
                place = pall_ref.at[pl.ds(p_place(lax.rem(y - sign * s + NY, NY)) + lane * piece, piece)]
                name = ("pg", sign, lane, s)
                message(
                    name, "y+" if sign > 0 else "y-", piece * ROWS * outs * 2,
                    lambda place=place, sign=sign: [(place, place, at_y(sign))],
                )
                p_filled[(-sign * (s + 1)) % NY].append(name)
                if s == 0:
                    p_goes.append(name)
                else:
                    tasks[("pgo", sign, lane, s)] = Task([("pg", sign, lane, s - 1)], [name], after=["pfin"])
    for off in range(NY):
        place = pall_ref.at[pl.ds(p_place(lax.rem(y + off, NY)), NZ)]
        message(("pd", off), "d", gr * outs * 2, lambda place=place: [(place, place, at_e(0, 1))])
    tasks["pgo"] = Task(["pgz"], [*p_goes, ("pd", 0)], after=["pfin"])
    for off in range(1, NY):
        tasks[("pdo", off)] = Task(p_filled[off], [("pd", off)], after=["pfin"])

    def own_place(dy):
        core = lax.rem(c + e // NZ, 2)
        return lax.rem(zh + lax.rem(e, NZ), NZ) * (NY * 2) + lax.rem(y + dy, NY) * 2 + core

    tile = 512
    for dy in range(NY):

        def project_in(dy=dy):
            part[...] = jnp.zeros_like(part)

            @pl.loop(0, feats // tile)
            def _(t):
                cols = pl.ds(pl.multiple_of(t * tile, tile), tile)
                rows = abuf[dy, :, :, :, cols].reshape(2 * NZ * ROWS, tile)
                part[...] += lax.dot_general(
                    rows, bbuf[:, cols], (((1,), (1,)), ((), ())), preferred_element_type=F32
                )

            mine[dy] = part[pl.ds(pl.multiple_of(e * ROWS, ROWS), ROWS), :]
            rsend[dy] = part[...].reshape(NE, ROWS, width).astype(BF)

        def sum_in(dy=dy):
            total = mine[dy]
            for k in range(NE - 1):
                total = total + rbuf[dy, k].astype(F32)
            pi_ref[own_place(dy)] = total.astype(BF)

        message(
            ("rs", dy), "x", 8 * ROWS * width,
            lambda dy=dy: [
                (rsend.at[dy, lax.rem(e + k, NE)], rbuf.at[dy, k - 1], at_e(k)) for k in range(1, NE)
            ],
            rbuf.at[dy],
        )
        message(
            ("ag", dy), "x", 8 * ROWS * width,
            lambda dy=dy: [
                (pi_ref.at[own_place(dy)], pi_ref.at[own_place(dy)], at_e(k)) for k in range(1, NE)
            ],
            pi_ref.at[pl.ds(0, NE - 1)],
        )
        shared = [("share", color, dy) for color in range(2)]
        tasks[("mm", dy)] = Task(
            [("d", 0, dy), ("d", 1, dy)], [("rs", dy)], project_in, 1.0, ["place", *shared], rank=3
        )
        tasks[("sum", dy)] = Task([("rs", dy)], [("ag", dy)], sum_in, 0.2, [("mm", dy)], rank=2)

    def begin():
        abuf[0, 0, 0] = a_ref[...]
        gbuf[pl.ds(pl.multiple_of(e * gr, gr), gr), pl.ds(0, gk)] = g_ref[pl.ds(pl.multiple_of(c * gr, gr), gr), :]
        bobuf[pl.ds(0, gk), :] = bo_ref[...]

    tasks["start"] = Task([], ["g", "bo", *own_sends])
    tasks["place"] = Task([], [], begin, 0.3, ["start"], rank=-1)
    for name, task in tasks.items():
        if name != "start" and not task.needs and not task.after:
            task.after = ["start"]

    waited = set()
    started = []

    def wait_for(name):
        if name in waited:
            return
        waited.add(name)
        item = messages[name]
        if item.whole is None:
            item.copies[0].wait_recv()
        else:
            ref, index = item.whole
            pltpu.make_async_copy(ref, ref, rsem.at[index]).wait()

    loaded = False
    for is_task, name in ordered(tasks, messages):
        if not is_task:
            item = messages[name]
            item.copies = item.make()
            for copy in item.copies:
                copy.start()
            started.append(item)
            continue
        task = tasks[name]
        for m in task.needs:
            wait_for(m)
        if name[0] == "mm" and not loaded:
            load_b.wait()
            loaded = True
        if task.run is not None:
            task.run()
    for name in messages:
        wait_for(name)
    combine(ids_ref, pall_ref, pi_ref, out_ref)
    for item in started:
        for copy in item.copies:
            copy.wait_send()


def combine(ids_ref, pout_ref, pin_ref, out_ref):
    blocks = pin_ref.shape[0]
    window = MOST // ROWS + 1
    ids = ids_ref[...]
    bounds = [jnp.sum((ids < n).astype(jnp.int32)) for n in range(NE + 1)]
    for n in range(NE):
        begin, end = bounds[n], bounds[n + 1]
        start = jnp.minimum(begin // ROWS, blocks - window)
        place = start * ROWS + lax.broadcasted_iota(jnp.int32, (window * ROWS, 1), 0)
        keep = (place >= begin) & (place < end)
        left = pout_ref[pl.ds(start, window)].reshape(window * ROWS, -1)
        right = pin_ref[pl.ds(start, window)].reshape(window * ROWS, -1)
        grad = lax.dot_general(
            right, jnp.where(keep, left, 0), (((0,), (0,)), ((), ())), preferred_element_type=F32
        )
        if n == 0:
            out_ref[...] = grad * grad
        elif n < NE - 1:
            out_ref[...] += grad * grad
        else:
            out_ref[...] = (out_ref[...] + grad * grad) * (1.0 / NE)


def local(activations, out_grads, basis_in, basis_out, example_ids):
    feats, width = basis_in.shape
    outs = basis_out.shape[1]
    tokens = example_ids.shape[0]
    gk = out_grads.shape[1]
    gr = out_grads.shape[0] // 2
    vmem = pl.BlockSpec(memory_space=pltpu.VMEM)
    wide1 = (feats * 22 // 28) // 256 * 256
    correction = pl.pallas_call(
        functools.partial(exchange, wide1),
        out_shape=jax.ShapeDtypeStruct((width, outs), F32),
        in_specs=[vmem, vmem, pl.BlockSpec(memory_space=pl.ANY), vmem, vmem],
        out_specs=vmem,
        scratch_shapes=[
            pltpu.VMEM((tokens // ROWS, ROWS, width), BF),
            pltpu.VMEM((tokens // ROWS, ROWS, outs), BF),
            pltpu.VMEM((NY, 2, NZ, ROWS, feats), BF),
            pltpu.VMEM((width, feats), BF),
            pltpu.VMEM((NE * gr, 2 * gk), BF),
            pltpu.VMEM((2 * gk, outs), BF),
            pltpu.VMEM((NY, gr, outs), F32),
            pltpu.VMEM((2, NY // 2, gr, outs), F32),
            pltpu.VMEM((NZ, ROWS, outs), F32),
            pltpu.VMEM((NZ - 1, ROWS, outs), F32),
            pltpu.VMEM((2 * NZ * ROWS, width), F32),
            pltpu.VMEM((NY, ROWS, width), F32),
            pltpu.VMEM((NY, NE, ROWS, width), BF),
            pltpu.VMEM((NY, NE - 1, ROWS, width), BF),
            pltpu.SemaphoreType.DMA((320,)),
            pltpu.SemaphoreType.DMA((240,)),
            pltpu.SemaphoreType.DMA((1,)),
        ],
        compiler_params=pltpu.CompilerParams(
            collective_id=0, has_side_effects=True, vmem_limit_bytes=60 << 20
        ),
        name="exchange",
    )(activations, out_grads, basis_in.T, basis_out, example_ids.reshape(-1, 128))
    return correction.T


def solution(mesh):
    finer = Mesh(mesh.devices.reshape(2, NX, NZ, NY, 2), AXES)
    placed = (P(BLK, EX), P(EX, BLK), P(EX, BLK), P(BLK, EX), P())
    return jax.shard_map(local, mesh=finer, in_specs=placed, out_specs=P(EX, BLK), check_vma=False)
```

time: 109 us -> 88.3 us (0.81)
  Pallas kernels: 100 us -> 86 us
  local copies, waits for them, and re-layouts: 9.04 us -> 2.16 us
    pallas_call x2 -> x1, Pallas kernels: 100 us -> 86 us  [local(): pl.pallas_call(functools.partial(exchange, wide1), out_shape=jax.ShapeDty...]
    unnamed x11 -> x1, local copies, waits for them, and re-layouts: 7.8 us -> 2.16 us
    pallas_call x1 -> x0, local copies, waits for them, and re-layouts: 1.24 us -> none  [local(): pl.pallas_call(combine, out_shape=jax.ShapeDtypeStruct((outs, width), F32...]
where the time goes in v2:
time: 88.3 us; the launch traced here: 88.1 us
  Pallas kernels  86 us (97%)
  local copies, waits for them, and re-layouts  2.16 us (2%)
    pallas_call x1, Pallas kernels, local(): pl.pallas_call(functools.partial(exchange, wide1), out_shape=jax.ShapeDty...  86 us
    unnamed x1, local copies, waits for them, and re-layouts  2.16 us

profile of v2, /device:TPU:1, one launch (start us, length us, event | category | flops | bytes accessed | tf_op | source)
XLA Modules:
  0.0 88.1 jit_solution(12110893210076266869)
XLA Ops:
  0.0 86.0 %exchange.1 = f32[448,512]{1,0:T(8,128)} custom-call(bf16[16,3584]{1,0:T(8,128)(2,1)} %a_ref.1, bf16[128,128]{1,0:T(8,128)(2,1)} %g_ref.1, bf16[448,3584]{1,0:T(8,128)(2,1)} %bitcast.4, bf16[128,512]{1,0:T(8,128)(2,1)} %bo_ref.1, s32[8,128]{1,0:T(8,128)} %bitcast.5), custom_call_target="tpu_custom_call" | custom-call | tf_op jit(solution)/shard_map/exchange/pallas_call | solution.py:434
  86.0 2.2 %copy.7 = f32[512,448]{0,1:T(8,128)} copy(f32[512,448]{0,1:T(8,128)} %bitcast.3) | data formatting | bytes 1835008

commit v3 on v2

--- a/solution.py
+++ b/solution.py
@@ -18,7 +18,7 @@
 BF = jnp.bfloat16
 F32 = jnp.float32
 
-RATE = {"y+": 40e3, "y-": 40e3, "z+": 16e3, "z-": 16e3, "x": 46e3, "d": 600e3}
+RATE = {"y+": 36e3, "y-": 36e3, "z+": 16e3, "z-": 16e3, "x": 46e3, "d": 600e3}
 LAG = {"y+": 3.0, "y-": 3.0, "z+": 4.0, "z-": 4.0, "x": 5.0, "d": 2.0}
 BACKLOG = 1.0
 

time: 88.3 us -> 90.7 us (1.027)
  Pallas kernels: 86 us -> 88.3 us
    pallas_call x1, Pallas kernels: 86 us -> 88.3 us  [local(): pl.pallas_call(functools.partial(exchange, wide1), out_shape=jax.ShapeDty...]
where the time goes in v3:
time: 90.7 us; the launch traced here: 90.5 us
  Pallas kernels  88.3 us (97%)
  local copies, waits for them, and re-layouts  2.16 us (2%)
    pallas_call x1, Pallas kernels, local(): pl.pallas_call(functools.partial(exchange, wide1), out_shape=jax.ShapeDty...  88.3 us
    unnamed x1, local copies, waits for them, and re-layouts  2.16 us

profile of v3, /device:TPU:1, one launch (start us, length us, event | category | flops | bytes accessed | tf_op | source)
XLA Modules:
  0.0 90.5 jit_solution(9252169367680789010)
XLA Ops:
  0.0 88.3 %exchange.1 = f32[448,512]{1,0:T(8,128)} custom-call(bf16[16,3584]{1,0:T(8,128)(2,1)} %a_ref.1, bf16[128,128]{1,0:T(8,128)(2,1)} %g_ref.1, bf16[448,3584]{1,0:T(8,128)(2,1)} %bitcast.4, bf16[128,512]{1,0:T(8,128)(2,1)} %bo_ref.1, s32[8,128]{1,0:T(8,128)} %bitcast.5), custom_call_target="tpu_custom_call" | custom-call | tf_op jit(solution)/shard_map/exchange/pallas_call | solution.py:434
  88.4 2.2 %copy.7 = f32[512,448]{0,1:T(8,128)} copy(f32[512,448]{0,1:T(8,128)} %bitcast.3) | data formatting | bytes 1835008
